TPU v7x, 512 devices: a whole 4x4x16 slice. The times are simulated.
512 devices in a mesh: expert: 128 (over z, y, core), token: 4 (over x).
Axes of the slice: x: 4, y: 4, z: 16, core: 2. Of those that a mesh axis runs over, the one named last changes fastest.
Arguments:
- tokens: bfloat16 [8192, 2048], P(('expert', 'token')), may hold values from -6 to 6
- routes: int32 [8192, 8], P(('expert', 'token')), may hold values from 0 to 127, all different within a row; in each aligned block of 16 rows (0 to 15, 16 to 31, ...) at most 2 rows name the same one
- assign: int32 [128], replicated, may hold values from 0 to 31, as said below
- gate_weight: bfloat16 [128, 2048, 1536], P('expert', None, 'token'), may hold values from -0.125 to 0.125
- up_weight: bfloat16 [128, 2048, 1536], P('expert', None, 'token'), may hold values from -0.125 to 0.125
- sketch: bfloat16 [128, 1536, 512], P('expert', 'token'), may hold values from -6 to 6
Outputs:
- hidden: bfloat16 [128, 1024, 1536], P('expert', None, 'token')
Inputs may be any that keep to these rules, and one draw needn't show every extreme that they name: `routes`: within each aligned block of 16 tokens each token names 8 different experts, and no expert is named by more than 2 entries of the block. `assign`: every one of the 32 clusters has at least two experts.
All inputs are finite; a program needn't handle non-finite values.
Results may differ from a plain program's by a relative error of at most 0.029.
Values may be sent and summed in bfloat16 or wider, within the bound.
A program may use at most 64 MiB of HBM per device.

v0:
```python
import jax
import jax.numpy as jnp
from jax import lax
from jax.sharding import PartitionSpec as P


def place_tokens(tok_rows, tok_ids, expert_count, capacity):
    flat_ids = tok_ids.reshape(-1)
    expert_hits = (flat_ids[:, None] == jnp.arange(expert_count, dtype=jnp.int32)[None, :]).astype(
        jnp.int32
    )
    earlier = jnp.cumsum(expert_hits, axis=0) - expert_hits
    slot_index = jnp.sum(earlier * expert_hits, axis=1)
    target = flat_ids * capacity + slot_index
    select = (
        jnp.arange(expert_count * capacity, dtype=jnp.int32)[:, None] == target[None, :]
    ).astype(jnp.float32)
    select = (
        select.reshape(expert_count * capacity, tok_rows.shape[0], tok_ids.shape[1])
        .sum(axis=2)
        .astype(jnp.bfloat16)
    )
    filled = jnp.dot(select, tok_rows, preferred_element_type=jnp.float32).astype(jnp.bfloat16)
    return filled.reshape(expert_count, capacity, tok_rows.shape[1])


def new_basis(partial_term, member, assign, token_count, expert_count):
    rank_cols = partial_term.shape[1]
    row_block = partial_term.shape[0] // (token_count * expert_count)
    pieces = partial_term.reshape(token_count, expert_count * row_block, rank_cols)
    arrived = lax.all_to_all(pieces, "expert", split_axis=1, concat_axis=1, tiled=True)
    arrived = arrived.reshape(token_count, expert_count, row_block, rank_cols)
    by_cluster = jnp.einsum("ci,tirk->ctrk", member, arrived, preferred_element_type=jnp.float32)
    own_rows = lax.psum_scatter(
        by_cluster.astype(jnp.bfloat16), "token", scatter_dimension=1, tiled=True
    ).astype(jnp.float32)
    outgoing = jnp.take(own_rows[:, 0], assign, axis=0).astype(jnp.bfloat16)
    returned = lax.all_to_all(outgoing, "expert", split_axis=0, concat_axis=0, tiled=True)
    cluster_rows = returned.reshape(expert_count * row_block, rank_cols)
    local_gram = lax.dot_general(
        cluster_rows, cluster_rows, (((0,), (0,)), ((), ())), preferred_element_type=jnp.float32
    )
    column_gram = lax.psum(local_gram.astype(jnp.bfloat16), "token").astype(jnp.float32)
    lower_factor = jnp.linalg.cholesky(column_gram)
    solved = jax.scipy.linalg.solve_triangular(
        lower_factor, cluster_rows.astype(jnp.float32).T, lower=True
    )
    basis_part = solved.T.astype(jnp.bfloat16)
    return lax.all_gather(basis_part, "token", axis=0, tiled=True)


def per_device(tokens, routes, assign, gate_weight, up_weight, sketch):
    expert_count = lax.axis_size("expert")
    token_count = lax.axis_size("token")
    cluster_count = expert_count // 4
    gate_local = gate_weight[0]
    up_local = up_weight[0]
    member = (assign[None, :] == jnp.arange(cluster_count, dtype=jnp.int32)[:, None]).astype(
        jnp.bfloat16
    )
    partial_term = jnp.dot(up_local, sketch[0], preferred_element_type=jnp.float32).astype(
        jnp.bfloat16
    )
    basis = new_basis(partial_term, member, assign, token_count, expert_count)
    projected = lax.dot_general(
        up_local, basis, (((0,), (0,)), ((), ())), preferred_element_type=jnp.float32
    ).astype(jnp.bfloat16)
    partial_term = jnp.dot(up_local, projected, preferred_element_type=jnp.float32).astype(
        jnp.bfloat16
    )
    basis = new_basis(partial_term, member, assign, token_count, expert_count)
    shard_rows = tokens.shape[0]
    capacity = max(2, 2 * shard_rows * routes.shape[1] // expert_count)
    outgoing = place_tokens(tokens, routes, expert_count, capacity)
    arrived = lax.all_to_all(outgoing, "expert", split_axis=0, concat_axis=0, tiled=True)
    slots_in = lax.all_gather(arrived, "token", axis=0, tiled=True)
    slots_in = slots_in.reshape(-1, tokens.shape[1])
    gate_value = jnp.dot(slots_in, gate_local, preferred_element_type=jnp.float32)
    on_basis = jnp.dot(slots_in, basis, preferred_element_type=jnp.float32).astype(jnp.bfloat16)
    coefficient = lax.dot_general(
        basis, up_local, (((0,), (0,)), ((), ())), preferred_element_type=jnp.float32
    ).astype(jnp.bfloat16)
    merged = jnp.dot(on_basis, coefficient, preferred_element_type=jnp.float32)
    hidden = (jax.nn.silu(gate_value) * merged).astype(jnp.bfloat16)
    return hidden[None]


def solution(mesh):
    return jax.shard_map(
        per_device,
        mesh=mesh,
        in_specs=(
            P(("expert", "token"), None),
            P(("expert", "token"), None),
            P(),
            P("expert", None, "token"),
            P("expert", None, "token"),
            P("expert", "token", None),
        ),
        out_specs=P("expert", None, "token"),
        check_vma=False,
    )
```

profile of v0, /device:TPU:1, one launch (start us, length us, event | category | flops | bytes accessed | tf_op | source)
XLA Modules:
  0.0 931.0 jit_solution(862876491536003445)
XLA Ops:
  7.9 2.2 convolution_convert_fusion.1
  11.8 117.2 %all_to_all.25 = bf16[4,512,512]{2,0,1:T(4,128)(2,1)S(1)} all-to-all(bf16[4,512,512]{2,0,1:T(4,128)(2,1)S(1)} %copy.53), channel_id=1, replica_groups=mesh['expert'=128,'token'=4] {'expert'}, dimensions={1} | all-to-all | bytes 4194304 | tf_op jit(solution)/shard_map/all_to_all | solution.py:31
  129.1 3.2 fusion.16
  132.4 22.3 %reduce-scatter.3.cloned.1.call-done = bf16[32,1,4,512]{3,0,2,1:T(8,128)(2,1)} async-done(((bf16[32,4,4,512]{3,0,2,1:T(8,128)(2,1)}), bf16[32,1,4,512]{3,0,2,1:T(8,128)(2,1)}) %reduce-scatter.3.cloned.1.call-update) | async-done | bytes 131088 | tf_op jit(solution)/shard_map/reduce_scatter | solution.py:34
  157.0 48.9 %all_to_all.26 = bf16[128,4,512]{2,1,0:T(4,128)(2,1)S(1)} all-to-all(bf16[128,4,512]{2,1,0:T(4,128)(2,1)S(1)} %select_convert_fusion.1), channel_id=1, replica_groups=mesh['expert'=128,'token'=4] {'expert'}, dimensions={0} | all-to-all | bytes 1048576 | tf_op jit(solution)/shard_map/all_to_all | solution.py:38
  208.9 47.0 %all-reduce.4.cloned.1.call-done = bf16[512,512]{0,1:T(8,128)(2,1)} async-done(((bf16[512,512]{0,1:T(8,128)(2,1)}), bf16[512,512]{0,1:T(8,128)(2,1)}) %all-reduce.4.cloned.1.call-update) | async-done | bytes 524304 | tf_op jit(solution)/shard_map/psum | solution.py:43
  259.4 11.7 %cholesky.286 = f32[128,128]{1,0:T(8,128)S(1)} custom-call(f32[128,128]{1,0:T(8,128)S(1)} %cholesky.426), custom_call_target="Cholesky" | custom-call | tf_op jit(solution)/shard_map/jit(cholesky)/cholesky | solution.py:44
  271.2 9.8 %custom-call.27 = f32[1,128,128]{1,2,0:T(8,128)S(1)} custom-call(f32[1,128,128]{2,1,0:T(8,128)S(1)} %get-tuple-element.63), custom_call_target="InvertDiagBlocksLowerTriangular" | custom-call | tf_op jit(solution)/shard_map/jit(cholesky)/cholesky | solution.py:44
  283.6 11.7 %cholesky.305 = f32[128,128]{1,0:T(8,128)S(1)} custom-call(f32[128,128]{1,0:T(8,128)S(1)} %cholesky.430), custom_call_target="Cholesky" | custom-call | tf_op jit(solution)/shard_map/jit(cholesky)/cholesky | solution.py:44
  295.4 10.0 %custom-call.28 = f32[1,128,128]{1,2,0:T(8,128)S(1)} custom-call(f32[1,128,128]{2,1,0:T(8,128)S(1)} %get-tuple-element.60), custom_call_target="InvertDiagBlocksLowerTriangular" | custom-call | tf_op jit(solution)/shard_map/jit(cholesky)/cholesky | solution.py:44
  307.0 11.7 %cholesky.326 = f32[128,128]{1,0:T(8,128)S(1)} custom-call(f32[128,128]{1,0:T(8,128)S(1)} %cholesky.435), custom_call_target="Cholesky" | custom-call | tf_op jit(solution)/shard_map/jit(cholesky)/cholesky | solution.py:44
  319.4 9.8 %custom-call.29 = f32[1,128,128]{1,2,0:T(8,128)S(1)} custom-call(f32[1,128,128]{2,1,0:T(8,128)S(1)} %get-tuple-element.57), custom_call_target="InvertDiagBlocksLowerTriangular" | custom-call | tf_op jit(solution)/shard_map/jit(cholesky)/cholesky | solution.py:44
  330.6 11.7 %cholesky.343 = f32[128,128]{1,0:T(8,128)S(1)} custom-call(f32[128,128]{1,0:T(8,128)S(1)} %convolution_subtract_fusion.11), custom_call_target="Cholesky" | custom-call | tf_op jit(solution)/shard_map/jit(cholesky)/cholesky | solution.py:44
  347.8 11.5 %while.4 = (s32[]{:T(128)}, f32[512,512]{1,0:T(8,128)}, s32[4,2]{0,1:T(2,128)S(1)}, f32[4,128,128]{2,1,0:T(8,128)S(1)}, s32[]{:T(128)}) while((s32[]{:T(128)}, f32[512,512]{1,0:T(8,128)}, s32[4,2]{0,1:T(2,128)S(1)}, f32[4,128,128]{2,1,0:T(8,128)S(1)}, s32[]{:T(128)}) %tuple.52), condition=%wide.while_cond, body=%wide.while_body.sunk | while | flops 2 | bytes 131189 | solution.py:45
  348.5 2.3 bitcast_dynamic-update-slice_fusion.4
  351.4 2.3 bitcast_dynamic-update-slice_fusion.4
  354.3 2.3 bitcast_dynamic-update-slice_fusion.4
  357.2 2.2 bitcast_dynamic-update-slice_fusion.4
  359.4 39.3 %custom-call.30 = f32[4,128,128]{1,2,0:T(8,128)S(1)} custom-call(f32[4,128,128]{2,1,0:T(8,128)S(1)} %get-tuple-element.22), custom_call_target="InvertDiagBlocksLowerTriangular" | custom-call | tf_op jit(solution)/shard_map/jit(_solve_triangular)/triangular_solve | solution.py:45
  406.5 41.5 %all-gather.6.cloned.1.call-done = bf16[2048,512]{0,1:T(8,128)(2,1)} async-done(((bf16[512,512]{0,1:T(8,128)(2,1)}), bf16[2048,512]{0,1:T(8,128)(2,1)}) %all-gather.6.cloned.1.call-update) | async-done | bytes 2097168 | tf_op jit(solution)/shard_map/all_gather | solution.py:49
  448.0 5.3 fusion
  453.3 4.5 reshape.84
  457.8 6.5 copy.61
  464.3 113.7 %all_to_all.27 = bf16[4,512,512]{2,0,1:T(4,128)(2,1)S(1)} all-to-all(bf16[4,512,512]{2,0,1:T(4,128)(2,1)} %copy.61), channel_id=1, replica_groups=mesh['expert'=128,'token'=4] {'expert'}, dimensions={1} | all-to-all | bytes 4194304 | tf_op jit(solution)/shard_map/all_to_all | solution.py:31
  578.0 3.2 fusion.19
  581.2 21.1 %reduce-scatter.5.cloned.1.call-done = bf16[32,1,4,512]{3,0,2,1:T(8,128)(2,1)} async-done(((bf16[32,4,4,512]{3,0,2,1:T(8,128)(2,1)}), bf16[32,1,4,512]{3,0,2,1:T(8,128)(2,1)}) %reduce-scatter.5.cloned.1.call-update) | async-done | bytes 131088 | tf_op jit(solution)/shard_map/reduce_scatter | solution.py:34
  605.5 18.3 %all-to-all-start.4 = ((bf16[128,4,512]{2,1,0:T(4,128)(2,1)}), bf16[128,4,512]{2,1,0:T(4,128)(2,1)S(1)}, u32[]{:S(2)}, u32[]{:S(2)}) async-start(bf16[128,4,512]{2,1,0:T(4,128)(2,1)} %select_convert_fusion), calls=%async_computation.6 | async-start | bytes 1048576 | tf_op jit(solution)/shard_map/all_to_all | solution.py:38
  626.6 28.0 %all-to-all-done.4 = bf16[128,4,512]{2,1,0:T(4,128)(2,1)S(1)} async-done(((bf16[128,4,512]{2,1,0:T(4,128)(2,1)}), bf16[128,4,512]{2,1,0:T(4,128)(2,1)S(1)}, u32[]{:S(2)}, u32[]{:S(2)}) %all-to-all-start.4) | async-done | bytes 524320 | tf_op jit(solution)/shard_map/all_to_all | solution.py:38
  654.6 9.1 all-to-all-start
  665.1 50.4 %all-to-all-done = bf16[128,2,2048]{2,1,0:T(2,128)(2,1)S(1)} async-done(((bf16[128,2,2048]{2,1,0:T(2,128)(2,1)}), bf16[128,2,2048]{2,1,0:T(2,128)(2,1)S(1)}, u32[]{:S(2)}, u32[]{:S(2)}) %all-to-all-start) | async-done | bytes 1048608 | tf_op jit(solution)/shard_map/all_to_all | solution.py:75
  718.2 4.0 all-reduce.6.cloned.1.call-done
  725.7 11.7 %cholesky.358 = f32[128,128]{1,0:T(8,128)S(1)} custom-call(f32[128,128]{1,0:T(8,128)S(1)} %cholesky.439), custom_call_target="Cholesky" | custom-call | tf_op jit(solution)/shard_map/jit(cholesky)/cholesky | solution.py:44
  737.4 9.8 %custom-call.31 = f32[1,128,128]{1,2,0:T(8,128)S(1)} custom-call(f32[1,128,128]{2,1,0:T(8,128)S(1)} %get-tuple-element.53), custom_call_target="InvertDiagBlocksLowerTriangular" | custom-call | tf_op jit(solution)/shard_map/jit(cholesky)/cholesky | solution.py:44
  749.9 11.7 %cholesky.377 = f32[128,128]{1,0:T(8,128)S(1)} custom-call(f32[128,128]{1,0:T(8,128)S(1)} %cholesky.443), custom_call_target="Cholesky" | custom-call | tf_op jit(solution)/shard_map/jit(cholesky)/cholesky | solution.py:44
  761.7 10.2 %custom-call.32 = f32[1,128,128]{1,2,0:T(8,128)S(1)} custom-call(f32[1,128,128]{2,1,0:T(8,128)S(1)} %get-tuple-element.50), custom_call_target="InvertDiagBlocksLowerTriangular" | custom-call | tf_op jit(solution)/shard_map/jit(cholesky)/cholesky | solution.py:44
  773.4 11.7 %cholesky.398 = f32[128,128]{1,0:T(8,128)S(1)} custom-call(f32[128,128]{1,0:T(8,128)S(1)} %cholesky.448), custom_call_target="Cholesky" | custom-call | tf_op jit(solution)/shard_map/jit(cholesky)/cholesky | solution.py:44
  785.2 9.8 %custom-call.33 = f32[1,128,128]{1,2,0:T(8,128)S(1)} custom-call(f32[1,128,128]{2,1,0:T(8,128)S(1)} %get-tuple-element.47), custom_call_target="InvertDiagBlocksLowerTriangular" | custom-call | tf_op jit(solution)/shard_map/jit(cholesky)/cholesky | solution.py:44
  796.4 11.7 %cholesky.415 = f32[128,128]{1,0:T(8,128)S(1)} custom-call(f32[128,128]{1,0:T(8,128)S(1)} %convolution_subtract_fusion.10), custom_call_target="Cholesky" | custom-call | tf_op jit(solution)/shard_map/jit(cholesky)/cholesky | solution.py:44
  814.6 11.3 %while.5 = (s32[]{:T(128)}, f32[512,512]{1,0:T(8,128)}, s32[4,2]{0,1:T(2,128)S(1)}, f32[4,128,128]{2,1,0:T(8,128)S(1)}, s32[]{:T(128)}) while((s32[]{:T(128)}, f32[512,512]{1,0:T(8,128)}, s32[4,2]{0,1:T(2,128)S(1)}, f32[4,128,128]{2,1,0:T(8,128)S(1)}, s32[]{:T(128)}) %tuple.72), condition=%wide.while_cond.clone, body=%wide.while_body.clone.sunk | while | flops 2 | bytes 131189 | solution.py:45
  815.2 2.2 bitcast_dynamic-update-slice_fusion.5
  818.0 2.2 bitcast_dynamic-update-slice_fusion.5
  820.9 2.2 bitcast_dynamic-update-slice_fusion.5
  825.9 39.3 %custom-call.34 = f32[4,128,128]{1,2,0:T(8,128)S(1)} custom-call(f32[4,128,128]{2,1,0:T(8,128)S(1)} %get-tuple-element.23), custom_call_target="InvertDiagBlocksLowerTriangular" | custom-call | tf_op jit(solution)/shard_map/jit(_solve_triangular)/triangular_solve | solution.py:45
  873.1 7.3 reshape.81
  880.4 5.7 fusion.11
  886.0 28.3 %all-gather.8.cloned.1.call-done = bf16[2048,512]{0,1:T(8,128)(2,1)} async-done(((bf16[512,512]{0,1:T(8,128)(2,1)}), bf16[2048,512]{0,1:T(8,128)(2,1)}) %all-gather.8.cloned.1.call-update) | async-done | bytes 2097168 | tf_op jit(solution)/shard_map/all_gather | solution.py:49
  914.3 2.8 fusion.25
  917.2 6.7 fusion.13
  (141 shorter events, 66.9 us)
Async XLA Ops:
  6.5 1.4 copy-start
  6.5 148.1 %reduce-scatter.3.cloned.1.call-start = ((), (), s32[]{:S(2)}) async-start(), calls=%async_computation.8 | async-start | bytes 655360 | tf_op jit(solution)/shard_map/reduce_scatter | solution.py:34
  11.8 117.2 %copy-start.8 = (s32[128]{0:T(128)S(1)}, s32[128]{0:T(128)}, u32[]{:S(2)}) copy-start(s32[128]{0:T(128)} %param.13) | copy-start | bytes 1540
  132.3 123.6 %all-reduce.4.cloned.1.call-start = ((), (), s32[]{:S(2)}) async-start(), calls=%async_computation.9 | async-start | bytes 1048576 | tf_op jit(solution)/shard_map/psum | solution.py:43
  207.3 240.8 %all-gather.6.cloned.1.call-start = ((), (), s32[]{:S(2)}) async-start(), calls=%async_computation.10 | async-start | bytes 2621440 | tf_op jit(solution)/shard_map/all_gather | solution.py:49
  258.4 1.0 copy-start.4
  347.8 54.0 %copy-start.2 = (f32[512,512]{0,1:T(8,128)S(1)}, f32[512,512]{0,1:T(8,128)}, u32[]{:S(2)}) copy-start(f32[512,512]{0,1:T(8,128)} %copy.60) | copy-start | bytes 3145732
  406.5 195.8 %reduce-scatter.5.cloned.1.call-start = ((), (), s32[]{:S(2)}) async-start(), calls=%async_computation.11 | async-start | bytes 655360 | tf_op jit(solution)/shard_map/reduce_scatter | solution.py:34
  581.2 42.6 %copy-start.7 = (s32[16,8]{0,1:T(8,128)S(1)}, s32[16,8]{0,1:T(8,128)}, u32[]{:S(2)}) copy-start(s32[16,8]{0,1:T(8,128)} %param.12) | copy-start | bytes 1540
  581.2 43.4 %copy-start.6 = (bf16[16,2048]{1,0:T(8,128)(2,1)S(1)}, bf16[16,2048]{1,0:T(8,128)(2,1)}, u32[]{:S(2)}) copy-start(bf16[16,2048]{1,0:T(8,128)(2,1)} %param.11) | copy-start | bytes 196612
  605.5 49.1 %all-to-all-start.4 = ((bf16[128,4,512]{2,1,0:T(4,128)(2,1)}), bf16[128,4,512]{2,1,0:T(4,128)(2,1)S(1)}, u32[]{:S(2)}, u32[]{:S(2)}) async-start(bf16[128,4,512]{2,1,0:T(4,128)(2,1)} %select_convert_fusion), calls=%async_computation.6 | async-start | bytes 1048576 | tf_op jit(solution)/shard_map/all_to_all | solution.py:38
  654.6 61.0 %all-to-all-start = ((bf16[128,2,2048]{2,1,0:T(2,128)(2,1)}), bf16[128,2,2048]{2,1,0:T(2,128)(2,1)S(1)}, u32[]{:S(2)}, u32[]{:S(2)}) async-start(bf16[128,2,2048]{2,1,0:T(2,128)(2,1)} %reshape.80), calls=%async_computation | async-start | bytes 2097152 | tf_op jit(solution)/shard_map/all_to_all | solution.py:75
  663.7 58.5 %all-reduce.6.cloned.1.call-start = ((), (), s32[]{:S(2)}) async-start(), calls=%async_computation.12 | async-start | bytes 1048576 | tf_op jit(solution)/shard_map/psum | solution.py:43
  665.1 208.0 %all-gather.4.cloned.1.call-start = ((), (), s32[]{:S(2)}) async-start(), calls=%async_computation.7 | async-start | bytes 5242880 | tf_op jit(solution)/shard_map/all_gather | solution.py:76
  715.5 1.0 copy-start.1
  716.5 197.8 %all-gather.8.cloned.1.call-start = ((), (), s32[]{:S(2)}) async-start(), calls=%async_computation.13 | async-start | bytes 2621440 | tf_op jit(solution)/shard_map/all_gather | solution.py:49
  724.7 1.0 copy-start.5
  814.5 53.8 %copy-start.3 = (f32[512,512]{0,1:T(8,128)S(1)}, f32[512,512]{0,1:T(8,128)}, u32[]{:S(2)}) copy-start(f32[512,512]{0,1:T(8,128)} %copy.68) | copy-start | bytes 3145732
  873.0 7.4 copy-start.9
  886.0 31.1 %copy-start.10 = (f32[1024,384]{1,0:T(8,128)S(1)}, f32[1024,384]{1,0:T(8,128)}, u32[]{:S(2)}) copy-start(f32[1024,384]{1,0:T(8,128)} %fusion.11) | copy-start | bytes 4718596
Sparse Core Ops, SparseCore 0:
  132.4 22.2 reduce-scatter.2
  207.4 48.4 all-reduce.3
  406.6 41.3 all-gather.5
  581.3 20.9 reduce-scatter.4
  666.6 55.6 all-reduce.5
  724.2 58.8 all-gather.3
  873.1 41.1 all-gather.7
where the time goes:
time: 940 us; the launch traced here: 931 us
  blocking collectives  280 us (30%)
  other arithmetic  246 us (26%)
  waiting for transfers between devices  243 us (26%)
  local copies, waits for them, and re-layouts  58.5 us (6%)
  matrix products  56.9 us (6%)
  starting transfers between devices  28 us (3%)
  between operations  19.3 us (2%)
    all_to_all x2, blocking collectives, new_basis(): lax.all_to_all(pieces, 'expert', split_axis=1, concat_axis=1, tiled=True)  231 us
    another operation x29, other arithmetic, new_basis(): lower_factor = jnp.linalg.cholesky(column_gram)  159 us
    another operation x5, other arithmetic, new_basis(): jax.scipy.linalg.solve_triangular(lower_factor, cluster_rows.astype(jnp.f...  80.9 us
    all_gather x2, waiting for transfers between devices, new_basis(): return lax.all_gather(basis_part, 'token', axis=0, tiled=True)  69.8 us
    psum x2, waiting for transfers between devices, new_basis(): lax.psum(local_gram.astype(jnp.bfloat16), 'token').astype(jnp.float32)  51 us
    all_to_all x1, waiting for transfers between devices, per_device(): lax.all_to_all(outgoing, 'expert', split_axis=0, concat_axis=0, tiled=True)  50.4 us
    all_to_all x1, blocking collectives, new_basis(): lax.all_to_all(outgoing, 'expert', split_axis=0, concat_axis=0, tiled=True)  48.9 us
    reduce_scatter x2, waiting for transfers between devices, new_basis(): lax.psum_scatter(by_cluster.astype(jnp.bfloat16), 'token', scatter_dimens...  43.4 us
  transfers between devices with their start and end apart: 9, of which 8 were waited for; matrix products, arithmetic and copies ran while one was open for 18% of the time, Pallas kernels for 0%

commit v1 on v0

--- a/solution.py
+++ b/solution.py
@@ -2,6 +2,35 @@
 import jax.numpy as jnp
 from jax import lax
 from jax.sharding import PartitionSpec as P
+
+
+def put_works(field_in):
+    lower, newest, current_arr = (
+        jax.lax.psum(1, "token"),
+        jax.lax.axis_index("token"),
+        field_in.shape[0],
+    )
+    bank = list(map(lambda no: (no, (no + 1) % lower), range(lower)))
+    pool = list(map(lambda no: (no, (no - 1) % lower), range(lower)))
+    current_block = jnp.zeros(
+        (*field_in.shape[:0], lower * current_arr, *field_in.shape[1:]), field_in.dtype
+    )
+    field_out = opened = field_in
+    arr_now = lower // 2
+    current_block = lax.dynamic_update_slice_in_dim(
+        current_block, field_in, newest * current_arr, axis=0
+    )
+    for k in range(1, arr_now + 1):
+        field_out = jax.lax.ppermute(field_out, "token", bank)
+        current_block = lax.dynamic_update_slice_in_dim(
+            current_block, field_out, (newest - k) % lower * current_arr, axis=0
+        )
+        if k < lower - arr_now:
+            opened = jax.lax.ppermute(opened, "token", pool)
+            current_block = lax.dynamic_update_slice_in_dim(
+                current_block, opened, (newest + k) % lower * current_arr, axis=0
+            )
+    return current_block
 
 
 def place_tokens(tok_rows, tok_ids, expert_count, capacity):
@@ -46,7 +75,7 @@
         lower_factor, cluster_rows.astype(jnp.float32).T, lower=True
     )
     basis_part = solved.T.astype(jnp.bfloat16)
-    return lax.all_gather(basis_part, "token", axis=0, tiled=True)
+    return put_works(basis_part)
 
 
 def per_device(tokens, routes, assign, gate_weight, up_weight, sketch):

time: 940 us -> 920 us (0.979)
  waiting for transfers between devices: 243 us -> 193 us
  starting transfers between devices: 28 us -> 44.9 us
    all_gather x2 -> x0, waiting for transfers between devices: 69.8 us -> none  [new_basis(): return lax.all_gather(basis_part, 'token', axis=0, tiled=True)]
    ppermute x0 -> x6, waiting for transfers between devices: none -> 21.1 us  [the longest x4 21 us: put_works(): field_out = jax.lax.ppermute(field_out, 'token', bank)]
    ppermute x0 -> x6, starting transfers between devices: none -> 16.9 us  [the longest x2 8.62 us: put_works(): opened = jax.lax.ppermute(opened, 'token', pool)]
  transfers between devices with their start and end apart: 9 -> 13, of which waited for: 8 -> 9; matrix products, arithmetic and copies ran while one was open for 18% -> 19% of each run, Pallas kernels for 0% -> 0%
where the time goes in v1:
time: 920 us; the launch traced here: 908 us
  blocking collectives  284 us (31%)
  other arithmetic  244 us (27%)
  waiting for transfers between devices  193 us (21%)
  local copies, waits for them, and re-layouts  67 us (7%)
  matrix products  55.7 us (6%)
  starting transfers between devices  44.9 us (5%)
  between operations  19.5 us (2%)
    all_to_all x2, blocking collectives, new_basis(): lax.all_to_all(pieces, 'expert', split_axis=1, concat_axis=1, tiled=True)  235 us
    another operation x29, other arithmetic, new_basis(): lower_factor = jnp.linalg.cholesky(column_gram)  158 us
    another operation x5, other arithmetic, new_basis(): jax.scipy.linalg.solve_triangular(lower_factor, cluster_rows.astype(jnp.f...  80.9 us
    psum x2, waiting for transfers between devices, new_basis(): lax.psum(local_gram.astype(jnp.bfloat16), 'token').astype(jnp.float32)  51.2 us
    all_to_all x1, waiting for transfers between devices, per_device(): lax.all_to_all(outgoing, 'expert', split_axis=0, concat_axis=0, tiled=True)  50.2 us
    all_to_all x1, blocking collectives, new_basis(): lax.all_to_all(outgoing, 'expert', split_axis=0, concat_axis=0, tiled=True)  48.9 us
    reduce_scatter x2, waiting for transfers between devices, new_basis(): lax.psum_scatter(by_cluster.astype(jnp.bfloat16), 'token', scatter_dimens...  42.2 us
    all_to_all x1, waiting for transfers between devices, new_basis(): lax.all_to_all(outgoing, 'expert', split_axis=0, concat_axis=0, tiled=True)  28 us
  transfers between devices with their start and end apart: 13, of which 9 were waited for; matrix products, arithmetic and copies ran while one was open for 19% of the time, Pallas kernels for 0%

profile of v1, /device:TPU:1, one launch (start us, length us, event | category | flops | bytes accessed | tf_op | source)
XLA Modules:
  0.0 907.8 jit_solution(14689972462395443872)
XLA Ops:
  7.9 2.2 convolution_convert_fusion.1
  11.8 117.2 %all_to_all.25 = bf16[4,512,512]{2,0,1:T(4,128)(2,1)S(1)} all-to-all(bf16[4,512,512]{2,0,1:T(4,128)(2,1)S(1)} %copy.53), channel_id=1, replica_groups=mesh['expert'=128,'token'=4] {'expert'}, dimensions={1} | all-to-all | bytes 4194304 | tf_op jit(solution)/shard_map/all_to_all | solution.py:60
  129.1 3.2 fusion.16
  132.4 22.3 %reduce-scatter.3.cloned.1.call-done = bf16[32,1,4,512]{3,0,2,1:T(8,128)(2,1)} async-done(((bf16[32,4,4,512]{3,0,2,1:T(8,128)(2,1)}), bf16[32,1,4,512]{3,0,2,1:T(8,128)(2,1)}) %reduce-scatter.3.cloned.1.call-update) | async-done | bytes 131088 | tf_op jit(solution)/shard_map/reduce_scatter | solution.py:63
  157.0 48.9 %all_to_all.26 = bf16[128,4,512]{2,1,0:T(4,128)(2,1)S(1)} all-to-all(bf16[128,4,512]{2,1,0:T(4,128)(2,1)S(1)} %select_convert_fusion.1), channel_id=1, replica_groups=mesh['expert'=128,'token'=4] {'expert'}, dimensions={0} | all-to-all | bytes 1048576 | tf_op jit(solution)/shard_map/all_to_all | solution.py:67
  208.9 47.0 %all-reduce.4.cloned.1.call-done = bf16[512,512]{0,1:T(8,128)(2,1)} async-done(((bf16[512,512]{0,1:T(8,128)(2,1)}), bf16[512,512]{0,1:T(8,128)(2,1)}) %all-reduce.4.cloned.1.call-update) | async-done | bytes 524304 | tf_op jit(solution)/shard_map/psum | solution.py:72
  259.4 11.7 %cholesky.286 = f32[128,128]{1,0:T(8,128)S(1)} custom-call(f32[128,128]{1,0:T(8,128)S(1)} %cholesky.426), custom_call_target="Cholesky" | custom-call | tf_op jit(solution)/shard_map/jit(cholesky)/cholesky | solution.py:73
  271.2 9.8 %custom-call.27 = f32[1,128,128]{1,2,0:T(8,128)S(1)} custom-call(f32[1,128,128]{2,1,0:T(8,128)S(1)} %get-tuple-element.67), custom_call_target="InvertDiagBlocksLowerTriangular" | custom-call | tf_op jit(solution)/shard_map/jit(cholesky)/cholesky | solution.py:73
  283.6 11.7 %cholesky.305 = f32[128,128]{1,0:T(8,128)S(1)} custom-call(f32[128,128]{1,0:T(8,128)S(1)} %cholesky.430), custom_call_target="Cholesky" | custom-call | tf_op jit(solution)/shard_map/jit(cholesky)/cholesky | solution.py:73
  295.4 10.0 %custom-call.28 = f32[1,128,128]{1,2,0:T(8,128)S(1)} custom-call(f32[1,128,128]{2,1,0:T(8,128)S(1)} %get-tuple-element.64), custom_call_target="InvertDiagBlocksLowerTriangular" | custom-call | tf_op jit(solution)/shard_map/jit(cholesky)/cholesky | solution.py:73
  307.0 11.7 %cholesky.326 = f32[128,128]{1,0:T(8,128)S(1)} custom-call(f32[128,128]{1,0:T(8,128)S(1)} %cholesky.435), custom_call_target="Cholesky" | custom-call | tf_op jit(solution)/shard_map/jit(cholesky)/cholesky | solution.py:73
  319.4 9.8 %custom-call.29 = f32[1,128,128]{1,2,0:T(8,128)S(1)} custom-call(f32[1,128,128]{2,1,0:T(8,128)S(1)} %get-tuple-element.61), custom_call_target="InvertDiagBlocksLowerTriangular" | custom-call | tf_op jit(solution)/shard_map/jit(cholesky)/cholesky | solution.py:73
  330.6 11.7 %cholesky.343 = f32[128,128]{1,0:T(8,128)S(1)} custom-call(f32[128,128]{1,0:T(8,128)S(1)} %convolution_subtract_fusion.11), custom_call_target="Cholesky" | custom-call | tf_op jit(solution)/shard_map/jit(cholesky)/cholesky | solution.py:73
  347.8 11.5 %while.4 = (s32[]{:T(128)}, f32[512,512]{1,0:T(8,128)}, s32[4,2]{0,1:T(2,128)S(1)}, f32[4,128,128]{2,1,0:T(8,128)S(1)}, s32[]{:T(128)}) while((s32[]{:T(128)}, f32[512,512]{1,0:T(8,128)}, s32[4,2]{0,1:T(2,128)S(1)}, f32[4,128,128]{2,1,0:T(8,128)S(1)}, s32[]{:T(128)}) %tuple.54), condition=%wide.while_cond, body=%wide.while_body.sunk | while | flops 2 | bytes 131181 | solution.py:74
  348.4 2.3 bitcast_dynamic-update-slice_fusion.4
  351.3 2.3 bitcast_dynamic-update-slice_fusion.4
  354.2 2.3 bitcast_dynamic-update-slice_fusion.4
  359.3 39.3 %custom-call.30 = f32[4,128,128]{1,2,0:T(8,128)S(1)} custom-call(f32[4,128,128]{2,1,0:T(8,128)S(1)} %get-tuple-element.22), custom_call_target="InvertDiagBlocksLowerTriangular" | custom-call | tf_op jit(solution)/shard_map/jit(_solve_triangular)/triangular_solve | solution.py:74
  407.3 2.3 collective-permute-start
  409.6 4.2 collective-permute-start.1
  413.8 7.2 collective-permute-done
  424.8 9.1 %collective-permute-done.2 = bf16[512,512]{0,1:T(8,128)(2,1)} collective-permute-done((bf16[512,512]{0,1:T(8,128)(2,1)S(1)}, bf16[512,512]{0,1:T(8,128)(2,1)}, u32[]{:S(2)}, u32[]{:S(2)}) %collective-permute-start.2) | collective-permute-done | bytes 524320 | tf_op jit(solution)/shard_map/ppermute | solution.py:24
  435.8 5.2 fusion
  441.0 4.5 reshape.84
  445.5 6.5 copy.61
  452.0 117.9 %all_to_all.27 = bf16[4,512,512]{2,0,1:T(4,128)(2,1)S(1)} all-to-all(bf16[4,512,512]{2,0,1:T(4,128)(2,1)} %copy.61), channel_id=1, replica_groups=mesh['expert'=128,'token'=4] {'expert'}, dimensions={1} | all-to-all | bytes 4194304 | tf_op jit(solution)/shard_map/all_to_all | solution.py:60
  569.9 3.2 fusion.19
  573.2 19.9 %reduce-scatter.5.cloned.1.call-done = bf16[32,1,4,512]{3,0,2,1:T(8,128)(2,1)} async-done(((bf16[32,4,4,512]{3,0,2,1:T(8,128)(2,1)}), bf16[32,1,4,512]{3,0,2,1:T(8,128)(2,1)}) %reduce-scatter.5.cloned.1.call-update) | async-done | bytes 131088 | tf_op jit(solution)/shard_map/reduce_scatter | solution.py:63
  596.2 18.3 %all-to-all-start.4 = ((bf16[128,4,512]{2,1,0:T(4,128)(2,1)}), bf16[128,4,512]{2,1,0:T(4,128)(2,1)S(1)}, u32[]{:S(2)}, u32[]{:S(2)}) async-start(bf16[128,4,512]{2,1,0:T(4,128)(2,1)} %select_convert_fusion), calls=%async_computation.6 | async-start | bytes 1048576 | tf_op jit(solution)/shard_map/all_to_all | solution.py:67
  617.4 28.0 %all-to-all-done.4 = bf16[128,4,512]{2,1,0:T(4,128)(2,1)S(1)} async-done(((bf16[128,4,512]{2,1,0:T(4,128)(2,1)}), bf16[128,4,512]{2,1,0:T(4,128)(2,1)S(1)}, u32[]{:S(2)}, u32[]{:S(2)}) %all-to-all-start.4) | async-done | bytes 524320 | tf_op jit(solution)/shard_map/all_to_all | solution.py:67
  645.4 9.1 %all-to-all-start = ((bf16[128,2,2048]{2,1,0:T(2,128)(2,1)}), bf16[128,2,2048]{2,1,0:T(2,128)(2,1)S(1)}, u32[]{:S(2)}, u32[]{:S(2)}) async-start(bf16[128,2,2048]{2,1,0:T(2,128)(2,1)} %reshape.80), calls=%async_computation | async-start | bytes 2097152 | tf_op jit(solution)/shard_map/all_to_all | solution.py:104
  656.1 50.2 %all-to-all-done = bf16[128,2,2048]{2,1,0:T(2,128)(2,1)S(1)} async-done(((bf16[128,2,2048]{2,1,0:T(2,128)(2,1)}), bf16[128,2,2048]{2,1,0:T(2,128)(2,1)S(1)}, u32[]{:S(2)}, u32[]{:S(2)}) %all-to-all-start) | async-done | bytes 1048608 | tf_op jit(solution)/shard_map/all_to_all | solution.py:104
  708.8 4.2 all-reduce.6.cloned.1.call-done
  716.5 11.7 %cholesky.358 = f32[128,128]{1,0:T(8,128)S(1)} custom-call(f32[128,128]{1,0:T(8,128)S(1)} %cholesky.439), custom_call_target="Cholesky" | custom-call | tf_op jit(solution)/shard_map/jit(cholesky)/cholesky | solution.py:73
  728.4 9.8 %custom-call.31 = f32[1,128,128]{1,2,0:T(8,128)S(1)} custom-call(f32[1,128,128]{2,1,0:T(8,128)S(1)} %get-tuple-element.57), custom_call_target="InvertDiagBlocksLowerTriangular" | custom-call | tf_op jit(solution)/shard_map/jit(cholesky)/cholesky | solution.py:73
  740.7 11.7 %cholesky.377 = f32[128,128]{1,0:T(8,128)S(1)} custom-call(f32[128,128]{1,0:T(8,128)S(1)} %cholesky.443), custom_call_target="Cholesky" | custom-call | tf_op jit(solution)/shard_map/jit(cholesky)/cholesky | solution.py:73
  752.4 10.2 %custom-call.32 = f32[1,128,128]{1,2,0:T(8,128)S(1)} custom-call(f32[1,128,128]{2,1,0:T(8,128)S(1)} %get-tuple-element.54), custom_call_target="InvertDiagBlocksLowerTriangular" | custom-call | tf_op jit(solution)/shard_map/jit(cholesky)/cholesky | solution.py:73
  764.2 11.7 %cholesky.398 = f32[128,128]{1,0:T(8,128)S(1)} custom-call(f32[128,128]{1,0:T(8,128)S(1)} %cholesky.448), custom_call_target="Cholesky" | custom-call | tf_op jit(solution)/shard_map/jit(cholesky)/cholesky | solution.py:73
  776.0 9.8 %custom-call.33 = f32[1,128,128]{1,2,0:T(8,128)S(1)} custom-call(f32[1,128,128]{2,1,0:T(8,128)S(1)} %get-tuple-element.51), custom_call_target="InvertDiagBlocksLowerTriangular" | custom-call | tf_op jit(solution)/shard_map/jit(cholesky)/cholesky | solution.py:73
  787.2 11.7 %cholesky.415 = f32[128,128]{1,0:T(8,128)S(1)} custom-call(f32[128,128]{1,0:T(8,128)S(1)} %convolution_subtract_fusion.10), custom_call_target="Cholesky" | custom-call | tf_op jit(solution)/shard_map/jit(cholesky)/cholesky | solution.py:73
  805.4 11.3 %while.5 = (s32[]{:T(128)}, f32[512,512]{1,0:T(8,128)}, s32[4,2]{0,1:T(2,128)S(1)}, f32[4,128,128]{2,1,0:T(8,128)S(1)}, s32[]{:T(128)}) while((s32[]{:T(128)}, f32[512,512]{1,0:T(8,128)}, s32[4,2]{0,1:T(2,128)S(1)}, f32[4,128,128]{2,1,0:T(8,128)S(1)}, s32[]{:T(128)}) %tuple.70), condition=%wide.while_cond.clone, body=%wide.while_body.clone.sunk | while | flops 2 | bytes 131181 | solution.py:74
  811.7 2.2 bitcast_dynamic-update-slice_fusion.5
  816.7 39.3 %custom-call.34 = f32[4,128,128]{1,2,0:T(8,128)S(1)} custom-call(f32[4,128,128]{2,1,0:T(8,128)S(1)} %get-tuple-element.23), custom_call_target="InvertDiagBlocksLowerTriangular" | custom-call | tf_op jit(solution)/shard_map/jit(_solve_triangular)/triangular_solve | solution.py:74
  866.8 7.2 reshape.81
  874.1 4.5 collective-permute-start.4
  880.5 6.1 fusion.11
  886.8 4.7 collective-permute-done.5
  894.3 6.7 fusion.13
  (161 shorter events, 87.3 us)
Async XLA Ops:
  6.5 1.4 copy-start
  6.5 148.1 %reduce-scatter.3.cloned.1.call-start = ((), (), s32[]{:S(2)}) async-start(), calls=%async_computation.8 | async-start | bytes 655360 | tf_op jit(solution)/shard_map/reduce_scatter | solution.py:63
  11.8 117.2 %copy-start.12 = (s32[128]{0:T(128)S(1)}, s32[128]{0:T(128)}, u32[]{:S(2)}) copy-start(s32[128]{0:T(128)} %param.13) | copy-start | bytes 1540
  132.3 123.6 %all-reduce.4.cloned.1.call-start = ((), (), s32[]{:S(2)}) async-start(), calls=%async_computation.9 | async-start | bytes 1048576 | tf_op jit(solution)/shard_map/psum | solution.py:72
  207.3 385.8 %reduce-scatter.5.cloned.1.call-start = ((), (), s32[]{:S(2)}) async-start(), calls=%async_computation.10 | async-start | bytes 655360 | tf_op jit(solution)/shard_map/reduce_scatter | solution.py:63
  258.4 1.0 copy-start.4
  347.8 54.0 %copy-start.2 = (f32[512,512]{0,1:T(8,128)S(1)}, f32[512,512]{0,1:T(8,128)}, u32[]{:S(2)}) copy-start(f32[512,512]{0,1:T(8,128)} %copy.60) | copy-start | bytes 3145732
  405.9 1.4 copy-start.9
  407.3 13.7 %collective-permute-start = (bf16[512,512]{0,1:T(8,128)(2,1)S(1)}, bf16[512,512]{0,1:T(8,128)(2,1)S(1)}, u32[]{:S(2)}, u32[]{:S(2)}) collective-permute-start(bf16[512,512]{0,1:T(8,128)(2,1)S(1)} %get-tuple-element.43), channel_id=1, source_target_pairs={{0,1},{1,2},{2,3},{3,0},{4,5},{5,6},{6,7},{7,4},{8,9},{9,10},{10,1... | collective-permute-start | bytes 1572872 | tf_op jit(solution)/shard_map/ppermute | solution.py:24
  409.6 14.2 %collective-permute-start.1 = (bf16[512,512]{0,1:T(8,128)(2,1)S(1)}, bf16[512,512]{0,1:T(8,128)(2,1)S(1)}, u32[]{:S(2)}, u32[]{:S(2)}) collective-permute-start(bf16[512,512]{0,1:T(8,128)(2,1)S(1)} %get-tuple-element.43), channel_id=1, source_target_pairs={{0,3},{1,0},{2,1},{3,2},{4,7},{5,4},{6,5},{7,6},{8,11},{9,8},{10,9... | collective-permute-start | bytes 1572872 | tf_op jit(solution)/shard_map/ppermute | solution.py:29
  421.0 12.9 %collective-permute-start.2 = (bf16[512,512]{0,1:T(8,128)(2,1)S(1)}, bf16[512,512]{0,1:T(8,128)(2,1)}, u32[]{:S(2)}, u32[]{:S(2)}) collective-permute-start(bf16[512,512]{0,1:T(8,128)(2,1)S(1)} %collective-permute-done), channel_id=1, source_target_pairs={{0,1},{1,2},{2,3},{3,0},{4,5},{5,6},{6,7},{7,4},{8,9},{9,10},{10,1... | collective-permute-start | bytes 1572872 | tf_op jit(solution)/shard_map/ppermute | solution.py:24
  573.1 41.4 %copy-start.11 = (s32[16,8]{0,1:T(8,128)S(1)}, s32[16,8]{0,1:T(8,128)}, u32[]{:S(2)}) copy-start(s32[16,8]{0,1:T(8,128)} %param.12) | copy-start | bytes 1540
  573.1 42.3 %copy-start.10 = (bf16[16,2048]{1,0:T(8,128)(2,1)S(1)}, bf16[16,2048]{1,0:T(8,128)(2,1)}, u32[]{:S(2)}) copy-start(bf16[16,2048]{1,0:T(8,128)(2,1)} %param.11) | copy-start | bytes 196612
  596.2 49.1 %all-to-all-start.4 = ((bf16[128,4,512]{2,1,0:T(4,128)(2,1)}), bf16[128,4,512]{2,1,0:T(4,128)(2,1)S(1)}, u32[]{:S(2)}, u32[]{:S(2)}) async-start(bf16[128,4,512]{2,1,0:T(4,128)(2,1)} %select_convert_fusion), calls=%async_computation.6 | async-start | bytes 1048576 | tf_op jit(solution)/shard_map/all_to_all | solution.py:67
  645.4 61.0 %all-to-all-start = ((bf16[128,2,2048]{2,1,0:T(2,128)(2,1)}), bf16[128,2,2048]{2,1,0:T(2,128)(2,1)S(1)}, u32[]{:S(2)}, u32[]{:S(2)}) async-start(bf16[128,2,2048]{2,1,0:T(2,128)(2,1)} %reshape.80), calls=%async_computation | async-start | bytes 2097152 | tf_op jit(solution)/shard_map/all_to_all | solution.py:104
  654.5 58.5 %all-reduce.6.cloned.1.call-start = ((), (), s32[]{:S(2)}) async-start(), calls=%async_computation.11 | async-start | bytes 1048576 | tf_op jit(solution)/shard_map/psum | solution.py:72
  655.8 211.0 %all-gather.2.cloned.1.call-start = ((), (), s32[]{:S(2)}) async-start(), calls=%async_computation.7 | async-start | bytes 5242880 | tf_op jit(solution)/shard_map/all_gather | solution.py:105
  706.3 1.0 copy-start.1
  715.5 1.0 copy-start.5
  805.3 53.8 %copy-start.3 = (f32[512,512]{0,1:T(8,128)S(1)}, f32[512,512]{0,1:T(8,128)}, u32[]{:S(2)}) copy-start(f32[512,512]{0,1:T(8,128)} %copy.68) | copy-start | bytes 3145732
  863.3 1.4 copy-start.6
  864.7 13.9 %collective-permute-start.3 = (bf16[512,512]{0,1:T(8,128)(2,1)S(1)}, bf16[512,512]{0,1:T(8,128)(2,1)S(1)}, u32[]{:S(2)}, u32[]{:S(2)}) collective-permute-start(bf16[512,512]{0,1:T(8,128)(2,1)S(1)} %get-tuple-element.41), channel_id=1, source_target_pairs={{0,1},{1,2},{2,3},{3,0},{4,5},{5,6},{6,7},{7,4},{8,9},{9,10},{10,1... | collective-permute-start | bytes 1572872 | tf_op jit(solution)/shard_map/ppermute | solution.py:24
  874.1 12.6 %copy-start.7 = (bf16[2048,512]{0,1:T(8,128)(2,1)S(1)}, bf16[2048,512]{0,1:T(8,128)(2,1)}, u32[]{:S(2)}) copy-start(bf16[2048,512]{0,1:T(8,128)(2,1)} %copy-done.6) | copy-start | bytes 6291460
  874.1 12.7 %collective-permute-start.4 = (bf16[512,512]{0,1:T(8,128)(2,1)S(1)}, bf16[512,512]{0,1:T(8,128)(2,1)S(1)}, u32[]{:S(2)}, u32[]{:S(2)}) collective-permute-start(bf16[512,512]{0,1:T(8,128)(2,1)S(1)} %get-tuple-element.41), channel_id=1, source_target_pairs={{0,3},{1,0},{2,1},{3,2},{4,7},{5,4},{6,5},{7,6},{8,11},{9,8},{10,9... | collective-permute-start | bytes 1572872 | tf_op jit(solution)/shard_map/ppermute | solution.py:29
  878.5 13.0 %collective-permute-start.5 = (bf16[512,512]{0,1:T(8,128)(2,1)S(1)}, bf16[512,512]{0,1:T(8,128)(2,1)S(1)}, u32[]{:S(2)}, u32[]{:S(2)}) collective-permute-start(bf16[512,512]{0,1:T(8,128)(2,1)S(1)} %collective-permute-done.3), channel_id=1, source_target_pairs={{0,1},{1,2},{2,3},{3,0},{4,5},{5,6},{6,7},{7,4},{8,9},{9,10},{10,1... | collective-permute-start | bytes 1572872 | tf_op jit(solution)/shard_map/ppermute | solution.py:24
  891.6 1.4 copy-start.8
  892.9 1.4 copy-start.13
Sparse Core Ops, SparseCore 0:
  132.4 22.2 reduce-scatter.2
  207.4 48.4 all-reduce.3
  573.3 19.7 reduce-scatter.4
  657.3 55.6 all-reduce.5
  714.9 59.0 all-gather.1
